TPU v7x, 32 devices: a whole 2x2x4 slice. The times are simulated.
32 devices in a mesh: depth: 8 (over y, x, core), screen: 4 (over z).
Axes of the slice: x: 2, y: 2, z: 4, core: 2. Of those that a mesh axis runs over, the one named last changes fastest.
Arguments:
- density: bfloat16 [80, 384, 2048], P('depth', 'screen'), may hold values from 0.099609375 to 10
- material: int32 [64, 384, 2048], P('depth', 'screen'), may hold values from 0 to 15
- order: int32 [8], replicated, may hold values from 0 to 7, each once
- color_table: float32 [16, 3], replicated, may hold values from 0.3 to 3
- extinction: float32 [16], replicated, may hold values from 0.015625 to 0.15625
Outputs:
- image: float32 [4, 384, 2048], P(None, ('screen', 'depth'))
Inputs may be any that keep to these rules, and one draw needn't show every extreme that they name: order is a permutation: each brick has a distinct rank.
All inputs are finite; a program needn't handle non-finite values.
Results may differ from a plain program's by a relative error of at most 0.0003.
Values may be sent and summed in bfloat16 or wider, within the bound.
A program may use at most 128 MiB of HBM per device.

v0:
```python
import jax
import jax.numpy as jnp
from jax import lax
from jax.sharding import PartitionSpec as P

light_x = 0.48
light_y = 0.6
light_z = 0.64


def with_halo(block, sides, width):
    for axis, dim in sides:
        count = lax.axis_size(axis)
        forward = [(i, i + 1) for i in range(count - 1)]
        backward = [(target, source) for source, target in forward]
        low = lax.ppermute(
            lax.slice_in_dim(block, block.shape[dim] - width, None, axis=dim), axis, forward
        )
        high = lax.ppermute(lax.slice_in_dim(block, 0, width, axis=dim), axis, backward)
        block = jnp.concatenate([low, block, high], axis=dim)
    return block


def lookup(kinds, table_column):
    picked = jnp.zeros(kinds.shape, jnp.float32)
    for entry in range(table_column.shape[0]):
        picked = jnp.where(kinds == entry, table_column[entry], picked)
    return picked


def body(density, material, order, color_table, extinction):
    with_rims = with_halo(density, (("screen", 1),), 1)
    float_full = with_rims.astype(jnp.float32)
    inner_rows = float_full[:, 1:-1]
    padded_x = jnp.pad(inner_rows, ((0, 0), (0, 0), (1, 1)))
    grad_z = 0.5 * (inner_rows[2:] - inner_rows[:-2])
    grad_y = 0.5 * (float_full[1:-1, 2:] - float_full[1:-1, :-2])
    grad_x = 0.5 * (padded_x[1:-1, :, 2:] - padded_x[1:-1, :, :-2])
    lit = light_x * grad_x + light_y * grad_y + light_z * grad_z
    shade = 0.55 + 0.45 * lit / jnp.sqrt(1.0 + grad_x * grad_x + grad_y * grad_y + grad_z * grad_z)
    rho = inner_rows[1:-1]
    extinct = lookup(material, extinction) * (rho / (1.0 + rho))
    ahead = jnp.cumsum(extinct, axis=0) - extinct
    weight = jnp.exp(-ahead) * (1.0 - jnp.exp(-extinct)) * shade
    red = jnp.sum(weight * lookup(material, color_table[:, 0]), axis=0)
    green = jnp.sum(weight * lookup(material, color_table[:, 1]), axis=0)
    blue = jnp.sum(weight * lookup(material, color_table[:, 2]), axis=0)
    optical = jnp.sum(extinct, axis=0)
    bricks = lax.axis_size("depth")
    rows = optical.shape[0]
    columns = optical.shape[1]
    strip_rows = rows // bricks
    before = (order[None, :] < order[:, None]).astype(jnp.float32)
    stacked = jnp.stack([red, green, blue, optical], axis=0).reshape(4, bricks, strip_rows, columns)
    strip_part = lax.all_to_all(stacked, "depth", split_axis=1, concat_axis=1, tiled=True)
    front_sum = jnp.einsum("kj,jrw->krw", before, strip_part[3], precision=lax.Precision.HIGHEST)
    attenuate = jnp.exp(-front_sum)
    colored = jnp.einsum(
        "ckrw,krw->crw", strip_part[:3], attenuate, precision=lax.Precision.HIGHEST
    )
    opacity_total = 1.0 - jnp.exp(-jnp.sum(strip_part[3], axis=0))
    return jnp.concatenate([colored, opacity_total[None]], axis=0)


def solution(mesh):
    placed = (P("depth", "screen", None), P("depth", "screen", None), P(), P(), P())
    return jax.shard_map(
        body,
        mesh=mesh,
        in_specs=placed,
        out_specs=P(None, ("screen", "depth"), None),
        check_vma=False,
    )
```

profile of v0, /device:TPU:0, one launch (start us, length us, event | category | flops | bytes accessed | tf_op | source)
XLA Modules:
  0.0 209.0 jit_solution(15220641258937264766)
XLA Ops:
  0.0 1.2 fusion.12
  1.2 4.9 %collective-permute-start = (bf16[10,1,2048]{2,1,0:T(2,128)(2,1)S(1)}, bf16[10,1,2048]{2,1,0:T(2,128)(2,1)S(1)}, u32[]{:S(2)}, u32[]{:S(2)}) collective-permute-start(bf16[10,1,2048]{2,1,0:T(2,128)(2,1)S(1)} %get-tuple-element.25), channel_id=1, source_target_pairs={{0,1},{1,2},{2,3},{4,5},{5,6},{6,7},{8,9},{9,10},{10,11},{12,13},{... | collective-permute-start | bytes 122888 | tf_op jit(solution)/shard_map/ppermute | solution.py:16
  6.1 1.3 collective-permute-start.1
  7.4 2.1 %fusion.15 = (f32[1,1]{0,1:T(1,128)}, f32[1,1]{0,1:T(1,128)}, f32[1,1]{0,1:T(1,128)}, f32[1,1]{0,1:T(1,128)}, f32[1,1]{0,1:T(1,128)}, /*index=5*/f32[1,1]{0,1:T(...) fusion(f32[16,3]{0,1:T(4,128)} %param.8), kind=kLoop, calls=%fused_computation.47 | loop fusion | bytes 152 | tf_op jit(solution)/shard_map/slice | solution.py:27
  9.6 2.1 %fusion.14 = (f32[1,1]{0,1:T(1,128)}, f32[1,1]{0,1:T(1,128)}, f32[1,1]{0,1:T(1,128)}, f32[1,1]{0,1:T(1,128)}, f32[1,1]{0,1:T(1,128)}, /*index=5*/f32[1,1]{0,1:T(...) fusion(f32[16,3]{0,1:T(4,128)} %param.8), kind=kLoop, calls=%fused_computation.46 | loop fusion | bytes 152 | tf_op jit(solution)/shard_map/slice | solution.py:27
  11.7 2.0 fusion.17
  13.6 1.7 fusion.16
  15.4 3.1 %maximum_convert_fusion = f32[10,98,2048]{2,1,0:T(8,128)S(1)} fusion(bf16[10,1,2048]{2,1,0:T(2,128)(2,1)S(1)} %collective-permute-done.1, bf16[10,96,2048]{2,1,0:T(8,128)(2,1)} %param.5, bf16[10,1,2048]{2,1,0:T(2,128)(2,1)S(1)} %collective-permute-done), kind=kLoop, calls=%fused_computation.11 | loop fusion | flops 12042240 | bytes 12042240 | tf_op jit(solution)/shard_map/convert_element_type | solution.py:33
  18.4 4.7 %slice.408 = f32[10,96,2048]{2,1,0:T(8,128)} slice(f32[10,98,2048]{2,1,0:T(8,128)S(1)} %maximum_convert_fusion), slice={[0:10], [1:97], [0:2048]} | slice | bytes 15728640 | tf_op jit(solution)/shard_map/slice | solution.py:34
  24.1 35.2 %fusion.10 = (f32[96,2048]{1,0:T(8,128)}, f32[8,96,2048]{2,1,0:T(8,128)S(1)}, pred[8,96,2048]{2,1,0:T(8,128)(4,1)S(1)}, pred[8,96,2048]{2,1,0:T(8,128)(4,1)S(1)}...) fusion(f32[10,98,2048]{2,1,0:T(8,128)S(1)} %maximum_convert_fus, ...), kind=kLoop, calls=%fused_computation.43 | loop fusion | flops 56426496 | bytes 44826688 | tf_op jit(solution)/shard_map/reduce_sum | solution.py:48
  59.3 3.3 %fusion.18 = f32[8,96,2048]{2,1,0:T(8,128)} fusion(f32[8,96,2048]{2,1,0:T(8,128)S(1)} %get-tuple-element.8), kind=kOutput, calls=%fused_computation.50 | output fusion | flops 11010048 | bytes 12582912 | tf_op jit(solution)/shard_map/jit(cumsum)/reduce_window_sum | solution.py:43
  62.6 1.3 copy-done.1
  63.9 41.8 %multiply_reduce_fusion.2 = (f32[96,2048]{1,0:T(8,128)}, f32[8,96,2048]{2,1,0:T(8,128)}) fusion(pred[8,96,2048]{2,1,0:T(8,128)(4,1)} %get-tuple-element.24, pred[8,96,2048]{2,1,0:T(8,128)(4,1)} %get-tuple-element.23, pred[8,96,2048]{2,1,0:T(8,128)(4,1)} %get-tuple-element.22, pred[8,96,2048]{2,1,0:T(8,128)(4,1)} %get-tuple-element.21, ...), kind=kLoop, calls=%fused_computation.9 | loop fusion | flops 69009408 | bytes 77856832 | tf_op jit(solution)/shard_map/reduce_sum | solution.py:45
  105.7 23.9 %multiply_reduce_fusion.1 = f32[96,2048]{1,0:T(8,128)} fusion(f32[8,96,2048]{2,1,0:T(8,128)} %get-tuple-element.6, pred[8,96,2048]{2,1,0:T(8,128)(4,1)} %get-tuple-element.24, pred[8,96,2048]{2,1,0:T(8,128)(4,1)} %get-tuple-element.23, pred[8,96,2048]{2,1,0:T(8,128)(4,1)} %get-tuple-element.22, pred[8,96,2048]{2,1,0:T(8,128)(4,1)} %get-tuple-element.21, ...), kind=kLoop, calls=%fused_computation.8 | loop fusion | flops 28114944 | bytes 32243776 | tf_op jit(solution)/shard_map/reduce_sum | solution.py:46
  129.5 2.2 %stack.16 = f32[1,8,12,2048]{3,2,1,0:T(8,128)} reshape(f32[96,2048]{1,0:T(8,128)} %multiply_reduce_fusion.1) | data formatting | bytes 1572864 | tf_op jit(solution)/shard_map/stack | solution.py:54
  131.8 23.9 %multiply_reduce_fusion = f32[96,2048]{1,0:T(8,128)} fusion(f32[8,96,2048]{2,1,0:T(8,128)} %get-tuple-element.6, pred[8,96,2048]{2,1,0:T(8,128)(4,1)} %get-tuple-element.24, pred[8,96,2048]{2,1,0:T(8,128)(4,1)} %get-tuple-element.23, pred[8,96,2048]{2,1,0:T(8,128)(4,1)} %get-tuple-element.22, pred[8,96,2048]{2,1,0:T(8,128)(4,1)} %get-tuple-element.21, ...), kind=kLoop, calls=%fused_computation.7 | loop fusion | flops 28114944 | bytes 32243776 | tf_op jit(solution)/shard_map/reduce_sum | solution.py:47
  155.7 1.2 stack.17
  156.9 1.2 stack.15
  158.1 1.2 stack.18
  159.4 1.5 pad_maximum_fusion
  160.9 2.0 copy.7
  162.9 41.4 %all_to_all.5 = f32[4,8,12,2048]{3,0,2,1:T(4,128)S(1)} all-to-all(f32[4,8,12,2048]{3,0,2,1:T(4,128)S(1)} %copy.7), channel_id=1, replica_groups=mesh['depth'=8,'screen'=4] {'depth'}, dimensions={1} | all-to-all | bytes 6291456 | tf_op jit(solution)/shard_map/all_to_all | solution.py:55
  204.3 1.2 fusion.13
  207.1 1.0 fusion.3
  (12 shorter events, 3.4 us)
Async XLA Ops:
  1.2 14.1 %collective-permute-start = (bf16[10,1,2048]{2,1,0:T(2,128)(2,1)S(1)}, bf16[10,1,2048]{2,1,0:T(2,128)(2,1)S(1)}, u32[]{:S(2)}, u32[]{:S(2)}) collective-permute-start(bf16[10,1,2048]{2,1,0:T(2,128)(2,1)S(1)} %get-tuple-element.25), channel_id=1, source_target_pairs={{0,1},{1,2},{2,3},{4,5},{5,6},{6,7},{8,9},{9,10},{10,11},{12,13},{... | collective-permute-start | bytes 122888 | tf_op jit(solution)/shard_map/ppermute | solution.py:16
  6.1 9.2 %collective-permute-start.1 = (bf16[10,1,2048]{2,1,0:T(2,128)(2,1)S(1)}, bf16[10,1,2048]{2,1,0:T(2,128)(2,1)S(1)}, u32[]{:S(2)}, u32[]{:S(2)}) collective-permute-start(bf16[10,1,2048]{2,1,0:T(2,128)(2,1)S(1)} %get-tuple-element.26), channel_id=1, source_target_pairs={{1,0},{2,1},{3,2},{5,4},{6,5},{7,6},{9,8},{10,9},{11,10},{13,12},{... | collective-permute-start | bytes 122888 | tf_op jit(solution)/shard_map/ppermute | solution.py:19
  18.4 5.6 %copy-start = (f32[10,98,2048]{2,1,0:T(8,128)}, f32[10,98,2048]{2,1,0:T(8,128)S(1)}, u32[]{:S(2)}) copy-start(f32[10,98,2048]{2,1,0:T(8,128)S(1)} %maximum_convert_fusion) | copy-start | bytes 24084484
  59.3 4.6 %copy-start.1 = (f32[8,96,2048]{2,1,0:T(8,128)}, f32[8,96,2048]{2,1,0:T(8,128)S(1)}, u32[]{:S(2)}) copy-start(f32[8,96,2048]{2,1,0:T(8,128)S(1)} %get-tuple-element.8) | copy-start | bytes 18874372
  160.9 44.6 %copy-start.2 = (s32[8]{0:T(128)S(1)}, s32[8]{0:T(128)}, u32[]{:S(2)}) copy-start(s32[8]{0:T(128)} %param.7) | copy-start | bytes 100
where the time goes:
time: 210 us; the launch traced here: 209 us
  other arithmetic  136 us (65%)
  blocking collectives  41.4 us (20%)
  local copies, waits for them, and re-layouts  24.5 us (12%)
  starting transfers between devices  6.22 us (3%)
    reduce_sum x1, other arithmetic, body(): red = jnp.sum(weight * lookup(material, color_table[:, 0]), axis=0)  41.8 us
    all_to_all x1, blocking collectives, body(): lax.all_to_all(stacked, 'depth', split_axis=1, concat_axis=1, tiled=True)  41.4 us
    reduce_sum x1, other arithmetic, body(): optical = jnp.sum(extinct, axis=0)  35.2 us
    reduce_sum x1, other arithmetic, body(): blue = jnp.sum(weight * lookup(material, color_table[:, 2]), axis=0)  23.9 us
    reduce_sum x1, other arithmetic, body(): green = jnp.sum(weight * lookup(material, color_table[:, 1]), axis=0)  23.9 us
    another operation x5, local copies, waits for them, and re-layouts, body(): jnp.stack([red, green, blue, optical], axis=0)  7.9 us
    slice x4, local copies, waits for them, and re-layouts, lookup(): picked = jnp.where(kinds == entry, table_column[entry], picked)  7.89 us
    ppermute x1, starting transfers between devices, with_halo(): lax.ppermute(lax.slice_in_dim(block, block.shape[dim] - width, None, axis...  4.93 us
  transfers between devices with their start and end apart: 2, of which 0 were waited for; matrix products, arithmetic and copies ran while one was open for 4% of the time, Pallas kernels for 0%

commit v1 on v0

v1 whole, which is shorter than its diff:
```python
import functools
import math
import jax
import jax.numpy as jnp
from jax import lax
from jax.experimental import pallas as pl
from jax.experimental.pallas import tpu as pltpu
from jax.sharding import PartitionSpec as P

LIGHT = (0.48, 0.6, 0.64)
MESH = pl.DeviceIdType.MESH
LANES = 128
CODE_TOP = 65000.0
CHUNKS = 2


def kernel(
    bricks, screens, strip,
    dens_hbm, mat_hbm, order_ref, color_ref, ext_ref, out_ref,
    dens, full, mat, sendbuf, recv, halo_out, halo_in,
    dens_sem, mat_sem, halo_send, halo_recv, send_sem, recv_sem, own_sem,
):
    stored, rows, cols = dens.shape
    slices = stored - 2
    unit = math.lcm(8, strip)
    units = rows // unit
    groups = unit // 8
    per_unit = unit // strip
    part = sendbuf.shape[2]
    blocks = strip // part
    entries = ext_ref.shape[0]

    me = lax.axis_index("depth")
    scr = lax.axis_index("screen")
    has_low = scr > 0
    has_high = scr < screens - 1

    own = (me * strip) // unit
    if units == 4:
        visits = [3 - own, own + 1 - 2 * (own % 2), (own + 2) % 4, own]
    else:
        visits = [(own + 1 + j) % units for j in range(units)]

    def dens_copy(h):
        half = rows // 2
        return pltpu.make_async_copy(
            dens_hbm.at[:, pl.ds(h * half, half)],
            dens.at[:, pl.ds(h * half, half)],
            dens_sem.at[h],
        )

    def mat_copy(j):
        where = pl.ds(pl.multiple_of(visits[j] * unit, 8), unit)
        return pltpu.make_async_copy(mat_hbm.at[:, where], mat.at[:, where], mat_sem.at[j])

    for h in range(2):
        dens_copy(h).start()
    for j in range(units):
        mat_copy(j).start()

    barrier = pltpu.get_barrier_semaphore()
    for peer in range(bricks):
        @pl.when(me != peer)
        def _():
            pl.semaphore_signal(barrier, inc=1, device_id=(peer, scr), device_id_type=MESH)

    @pl.when(has_low)
    def _():
        pl.semaphore_signal(barrier, inc=1, device_id=(me, scr - 1), device_id_type=MESH)

    @pl.when(has_high)
    def _():
        pl.semaphore_signal(barrier, inc=1, device_id=(me, scr + 1), device_id_type=MESH)

    lane = lax.broadcasted_iota(jnp.int32, (8, LANES), 1)
    sub = lax.broadcasted_iota(jnp.int32, (8, LANES), 0)

    def table(read):
        out = jnp.zeros((8, LANES), jnp.float32)
        for e in range(entries):
            out = jnp.where(lane == e, read(e), out)
        return out

    tabs = [table(lambda e, c=c: color_ref[c, e]) for c in range(3)]
    ext2 = table(lambda e: ext_ref[e]) * math.log2(math.e)
    tops = [jnp.max(t, axis=1, keepdims=True) for t in tabs]
    top_tau = slices * jnp.max(ext2, axis=1, keepdims=True)
    steps = [jnp.broadcast_to(t * (1.0 / CODE_TOP), (8, LANES)) for t in tops + [top_tau]]
    scales = [1.0 / s for s in steps]

    for h in range(2):
        dens_copy(h).wait()

    for z in range(slices):
        halo_out[0, z : z + 1, :] = dens[z + 1, 0:16, :].astype(jnp.float32)[0:1]
        halo_out[1, z : z + 1, :] = dens[z + 1, rows - 16 : rows, :].astype(jnp.float32)[15:16]

    pl.semaphore_wait(
        barrier, bricks - 1 + jnp.where(has_low, 1, 0) + jnp.where(has_high, 1, 0)
    )

    def halo_copy(side):
        return pltpu.make_async_remote_copy(
            src_ref=halo_out.at[side],
            dst_ref=halo_in.at[1 - side],
            send_sem=halo_send.at[side],
            recv_sem=halo_recv.at[1 - side],
            device_id=(me, scr + 2 * side - 1),
            device_id_type=MESH,
        )

    def halo_wait(side):
        pltpu.make_async_remote_copy(
            src_ref=halo_out.at[side],
            dst_ref=halo_in.at[side],
            send_sem=halo_send.at[side],
            recv_sem=halo_recv.at[side],
            device_id=(me, scr + 2 * side - 1),
            device_id_type=MESH,
        ).wait_recv()

    @pl.when(has_low)
    def _():
        halo_copy(0).start()

    @pl.when(has_high)
    def _():
        halo_copy(1).start()

    @pl.loop(0, stored)
    def _(z):
        full[z, 8 : 8 + rows, 0:LANES] = jnp.zeros((rows, LANES), jnp.float32)
        full[z, 8 : 8 + rows, LANES + cols :] = jnp.zeros((rows, LANES), jnp.float32)

        @pl.loop(0, rows // 16)
        def _(i):
            r = pl.multiple_of(i * 16, 16)
            full[z, pl.ds(pl.multiple_of(r + 8, 8), 16), LANES : LANES + cols] = dens[
                z, pl.ds(r, 16), :
            ].astype(jnp.float32)

    def pixel_tile(r, c):
        def tile(z, dr, dc):
            return full[
                z,
                pl.ds(pl.multiple_of(r + 8 + dr * 8, 8), 8),
                pl.ds(pl.multiple_of(c + (1 + dc) * LANES, LANES), LANES),
            ]

        through = jnp.ones((8, LANES), jnp.float32)
        tau = jnp.zeros((8, LANES), jnp.float32)
        sums = [jnp.zeros((8, LANES), jnp.float32) for _ in range(3)]
        before, here = tile(0, 0, 0), tile(1, 0, 0)
        for z in range(slices):
            after = tile(z + 2, 0, 0)
            left = pltpu.roll(jnp.where(lane == LANES - 1, tile(z + 1, 0, -1), here), 1, 1)
            right = pltpu.roll(jnp.where(lane == 0, tile(z + 1, 0, 1), here), LANES - 1, 1)
            up = pltpu.roll(jnp.where(sub == 7, tile(z + 1, -1, 0), here), 1, 0)
            down = pltpu.roll(jnp.where(sub == 0, tile(z + 1, 1, 0), here), 7, 0)
            dx, dy, dz = right - left, down - up, after - before
            square = (dx * dx + dy * dy) + (dz * dz + 4.0)
            lit = (0.45 * LIGHT[0]) * dx + (0.45 * LIGHT[1]) * dy + (0.45 * LIGHT[2]) * dz
            shade = 0.55 + lit * lax.rsqrt(square)
            kinds = mat[z, pl.ds(r, 8), pl.ds(c, LANES)]

            def pick(values):
                return jnp.take_along_axis(values, kinds, axis=1, mode="promise_in_bounds")

            sigma = pick(ext2) * (here / (1.0 + here))
            later = through * jnp.exp2(-sigma)
            weight = (through - later) * shade
            for k in range(3):
                sums[k] = sums[k] + weight * pick(tabs[k])
            tau = tau + sigma
            through = later
            before, here = here, after
        gain = 1.0 / (1.0 - through)
        values = [s * gain for s in sums] + [tau]
        codes = [
            jnp.minimum(v * s + 0.5, 65535.0).astype(jnp.int32) for v, s in zip(values, scales)
        ]
        return [(codes[0] << 16) | codes[1], (codes[2] << 16) | codes[3]]

    def row_group(unit_at, g):
        r = pl.multiple_of(unit_at * unit + g * 8, 8)

        @pl.loop(0, cols // (LANES * CHUNKS))
        def _(i):
            for k in range(CHUNKS):
                c = pl.multiple_of(i * (LANES * CHUNKS) + k * LANES, LANES)
                words = pixel_tile(r, c)
                for p in range(2):
                    for h in range(8 // part):
                        sendbuf[
                            unit_at * (unit // part) + g * (8 // part) + h, p, :, pl.ds(c, LANES)
                        ] = words[p][h * part : (h + 1) * part]

    def strip_copy(s):
        return pltpu.make_async_remote_copy(
            src_ref=sendbuf.at[pl.ds(s * blocks, blocks)],
            dst_ref=recv.at[me],
            send_sem=send_sem.at[s],
            recv_sem=recv_sem.at[me],
            device_id=(s, scr),
            device_id_type=MESH,
        )

    def own_copy():
        return pltpu.make_async_copy(
            sendbuf.at[pl.ds(me * blocks, blocks)], recv.at[me], own_sem
        )

    def set_halo(side, there):
        row = 7 if side == 0 else 8 + rows

        @pl.when(there)
        def _():
            halo_wait(side)
            for z in range(slices):
                full[z + 1, row : row + 1, LANES : LANES + cols] = halo_in[side, z : z + 1, :]

        @pl.when(jnp.logical_not(there))
        def _():
            for z in range(slices):
                full[z + 1, row : row + 1, LANES : LANES + cols] = jnp.zeros(
                    (1, cols), jnp.float32
                )

    for j in range(units):
        at = visits[j]
        mat_copy(j).wait()

        @pl.loop(0, groups)
        def _(i):
            @pl.when(jnp.logical_and(i == groups - 1, at == 0))
            def _():
                set_halo(0, has_low)

            @pl.when(jnp.logical_and(i == groups - 1, at == units - 1))
            def _():
                set_halo(1, has_high)

            row_group(at, jnp.where(at == 0, groups - 1 - i, i))

        for k in range(per_unit):
            s = at * per_unit + k
            if j < units - 1:
                strip_copy(s).start()
            else:
                @pl.when(s != me)
                def _():
                    strip_copy(s).start()

                @pl.when(s == me)
                def _():
                    own_copy().start()

    def brick_at(rank):
        def step(j, found):
            return jnp.maximum(found, jnp.where(order_ref[j] == rank, j, 0))

        return lax.fori_loop(0, bricks, step, jnp.int32(0), unroll=bricks <= 8)

    at_rank = [brick_at(i) for i in range(bricks)]

    own_copy().wait()
    for peer in range(bricks):
        @pl.when(me != peer)
        def _():
            pltpu.make_async_remote_copy(
                src_ref=sendbuf.at[pl.ds(peer * blocks, blocks)],
                dst_ref=recv.at[peer],
                send_sem=send_sem.at[peer],
                recv_sem=recv_sem.at[peer],
                device_id=(peer, scr),
                device_id_type=MESH,
            ).wait_recv()

    width = 4 * LANES
    unscale = [jnp.concatenate([s[:part]] * (width // LANES), axis=1) for s in steps]
    for b in range(blocks):
        @pl.loop(0, cols // width)
        def _(i):
            where = pl.ds(pl.multiple_of(i * width, width), width)
            through = jnp.ones((part, width), jnp.float32)
            sums = [jnp.zeros((part, width), jnp.float32) for _ in range(3)]
            for rank in range(bricks):
                first = recv[at_rank[rank], b, 0, :, where]
                second = recv[at_rank[rank], b, 1, :, where]
                codes = []
                for word in (first, second):
                    codes += [lax.shift_right_logical(word, 16), word & 0xFFFF]
                values = [k.astype(jnp.float32) * s for k, s in zip(codes, unscale)]
                later = through * jnp.exp2(-values[3])
                weight = through - later
                sums = [a + weight * v for a, v in zip(sums, values[:3])]
                through = later
            for k, value in enumerate(sums + [1.0 - through]):
                out_ref[k, b * part : (b + 1) * part, where] = value

    for peer in range(bricks):
        @pl.when(me != peer)
        def _():
            strip_copy(peer).wait_send()

    @pl.when(has_low)
    def _():
        halo_copy(0).wait_send()

    @pl.when(has_high)
    def _():
        halo_copy(1).wait_send()


def solution(mesh):
    bricks, screens = mesh.shape["depth"], mesh.shape["screen"]

    def body(density, material, order, color_table, extinction):
        stored, rows, cols = density.shape
        slices = stored - 2
        strip = rows // bricks
        part = math.gcd(8, strip)
        blocks = strip // part
        smem = pl.BlockSpec(memory_space=pltpu.SMEM)
        hbm = pl.BlockSpec(memory_space=pl.ANY)
        voxels = slices * rows * cols
        return pl.pallas_call(
            functools.partial(kernel, bricks, screens, strip),
            out_shape=jax.ShapeDtypeStruct((4, strip, cols), jnp.float32),
            in_specs=[hbm, hbm, smem, smem, smem],
            out_specs=pl.BlockSpec(memory_space=pltpu.VMEM),
            scratch_shapes=[
                pltpu.VMEM((stored, rows, cols), jnp.bfloat16),
                pltpu.VMEM((stored, rows + 16, cols + 2 * LANES), jnp.float32),
                pltpu.VMEM((slices, rows, cols), jnp.int32),
                pltpu.VMEM((rows // part, 2, part, cols), jnp.int32),
                pltpu.VMEM((bricks, blocks, 2, part, cols), jnp.int32),
                pltpu.VMEM((2, slices, cols), jnp.float32),
                pltpu.VMEM((2, slices, cols), jnp.float32),
                pltpu.SemaphoreType.DMA((2,)),
                pltpu.SemaphoreType.DMA((rows // math.lcm(8, strip),)),
                pltpu.SemaphoreType.DMA((2,)),
                pltpu.SemaphoreType.DMA((2,)),
                pltpu.SemaphoreType.DMA((bricks,)),
                pltpu.SemaphoreType.DMA((bricks,)),
                pltpu.SemaphoreType.DMA,
            ],
            compiler_params=pltpu.CompilerParams(
                collective_id=0, has_side_effects=True, vmem_limit_bytes=48 * 1024 * 1024
            ),
            cost_estimate=pl.CostEstimate(
                flops=60 * voxels, bytes_accessed=7 * voxels, transcendentals=3 * voxels
            ),
        )(density, material, order, color_table.T, extinction)

    placed = (P("depth", "screen", None), P("depth", "screen", None), P(), P(), P())
    return jax.shard_map(
        body,
        mesh=mesh,
        in_specs=placed,
        out_specs=P(None, ("screen", "depth"), None),
        check_vma=False,
    )
```

time: 210 us -> 39.5 us (0.19)
  the two profiles are of different devices: /device:TPU:0 before, /device:TPU:1 now
where the time goes in v1:
time: 39.5 us; the launch traced here: 39.3 us
  Pallas kernels  34.2 us (87%)
  local copies, waits for them, and re-layouts  5.1 us (13%)
    pallas_call x1, Pallas kernels, body(): pl.pallas_call(functools.partial(kernel, bricks, screens, strip), out_sha...  34.2 us
    unnamed x8, local copies, waits for them, and re-layouts  4.1 us
    pallas_call x1, local copies, waits for them, and re-layouts, body(): pl.pallas_call(functools.partial(kernel, bricks, screens, strip), out_sha...  1 us

profile of v1, /device:TPU:1, one launch (start us, length us, event | category | flops | bytes accessed | tf_op | source)
XLA Modules:
  0.0 39.3 jit_solution(16539530197967295319)
XLA Ops:
  0.0 0.0 copy-start
  0.0 2.1 %copy-done = bf16[10,96,2048]{2,1,0:T(8,128)(2,1)S(1)} copy-done((bf16[10,96,2048]{2,1,0:T(8,128)(2,1)S(1)}, bf16[10,96,2048]{2,1,0:T(8,128)(2,1)}, u32[]{:S(2)}) %copy-start) | copy-done | bytes 3932184
  2.1 0.0 copy-start.1
  2.1 0.7 %copy-done.1 = f32[16,3]{0,1:T(4,128)S(1)} copy-done((f32[16,3]{0,1:T(4,128)S(1)}, f32[16,3]{0,1:T(4,128)}, u32[]{:S(2)}) %copy-start.1) | copy-done | bytes 216
  2.8 0.0 copy-start.2
  2.8 0.7 %copy-done.2 = s32[8]{0:T(128)S(1)} copy-done((s32[8]{0:T(128)S(1)}, s32[8]{0:T(128)}, u32[]{:S(2)}) %copy-start.2) | copy-done | bytes 56
  3.5 0.0 copy-start.3
  3.5 0.7 %copy-done.3 = f32[16]{0:T(128)S(1)} copy-done((f32[16]{0:T(128)S(1)}, f32[16]{0:T(128)}, u32[]{:S(2)}) %copy-start.3) | copy-done | bytes 88
  4.1 34.2 %shard_map.55 = f32[4,12,2048]{2,1,0:T(8,128)S(1)} custom-call(bf16[10,96,2048]{2,1,0:T(8,128)(2,1)S(1)} %copy-done, s32[8,96,2048]{2,1,0:T(8,128)} %mat_hbm.1, s32[8]{0:T(128)S(1)} %copy-done.2, f32[3,16]{1,0:T(4,128)S(1)} %bitcast.1, f32[16]{0:T(128)S(1)} %copy-done.3), custom_call_target="tpu_custom_call" | custom-call | flops 94371840 | bytes 11010048 | tf_op jit(solution)/shard_map/pallas_call | solution.py:327
  38.3 1.0 %copy.6 = f32[4,12,2048]{2,0,1:T(4,128)} copy(f32[4,12,2048]{2,1,0:T(8,128)S(1)} %shard_map.55) | data formatting | bytes 786432 | tf_op jit(solution)/shard_map/pallas_call | solution.py:327
Async XLA Ops:
  0.0 2.1 %copy-start = (bf16[10,96,2048]{2,1,0:T(8,128)(2,1)S(1)}, bf16[10,96,2048]{2,1,0:T(8,128)(2,1)}, u32[]{:S(2)}) copy-start(bf16[10,96,2048]{2,1,0:T(8,128)(2,1)} %dens_hbm.1) | copy-start | bytes 11796484
  2.1 0.7 %copy-start.1 = (f32[16,3]{0,1:T(4,128)S(1)}, f32[16,3]{0,1:T(4,128)}, u32[]{:S(2)}) copy-start(f32[16,3]{0,1:T(4,128)} %param.8) | copy-start | bytes 580
  2.8 0.7 %copy-start.2 = (s32[8]{0:T(128)S(1)}, s32[8]{0:T(128)}, u32[]{:S(2)}) copy-start(s32[8]{0:T(128)} %order_ref.1) | copy-start | bytes 100
  3.5 0.7 %copy-start.3 = (f32[16]{0:T(128)S(1)}, f32[16]{0:T(128)}, u32[]{:S(2)}) copy-start(f32[16]{0:T(128)} %ext_ref.1) | copy-start | bytes 196

commit v2 on v1

--- a/solution.py
+++ b/solution.py
@@ -11,14 +11,15 @@
 MESH = pl.DeviceIdType.MESH
 LANES = 128
 CODE_TOP = 65000.0
-CHUNKS = 2
+CHUNKS = 4
 
 
 def kernel(
     bricks, screens, strip,
-    dens_hbm, mat_hbm, order_ref, color_ref, ext_ref, out_ref,
+    dens_hbm, mat_hbm, order_hbm, color_hbm, ext_hbm, out_ref,
     dens, full, mat, sendbuf, recv, halo_out, halo_in,
     dens_sem, mat_sem, halo_send, halo_recv, send_sem, recv_sem, own_sem,
+    order_ref, color_ref, ext_ref, small_sem,
 ):
     stored, rows, cols = dens.shape
     slices = stored - 2
@@ -53,6 +54,14 @@
         where = pl.ds(pl.multiple_of(visits[j] * unit, 8), unit)
         return pltpu.make_async_copy(mat_hbm.at[:, where], mat.at[:, where], mat_sem.at[j])
 
+    small = [
+        pltpu.make_async_copy(src, dst, small_sem.at[i])
+        for i, (src, dst) in enumerate(
+            [(order_hbm, order_ref), (color_hbm, color_ref), (ext_hbm, ext_ref)]
+        )
+    ]
+    for copy in small:
+        copy.start()
     for h in range(2):
         dens_copy(h).start()
     for j in range(units):
@@ -71,6 +80,9 @@
     @pl.when(has_high)
     def _():
         pl.semaphore_signal(barrier, inc=1, device_id=(me, scr + 1), device_id_type=MESH)
+
+    for copy in small:
+        copy.wait()
 
     lane = lax.broadcasted_iota(jnp.int32, (8, LANES), 1)
     sub = lax.broadcasted_iota(jnp.int32, (8, LANES), 0)
@@ -94,6 +106,18 @@
     for z in range(slices):
         halo_out[0, z : z + 1, :] = dens[z + 1, 0:16, :].astype(jnp.float32)[0:1]
         halo_out[1, z : z + 1, :] = dens[z + 1, rows - 16 : rows, :].astype(jnp.float32)[15:16]
+
+    @pl.loop(0, stored)
+    def _(z):
+        full[z, 8 : 8 + rows, 0:LANES] = jnp.zeros((rows, LANES), jnp.float32)
+        full[z, 8 : 8 + rows, LANES + cols :] = jnp.zeros((rows, LANES), jnp.float32)
+
+        @pl.loop(0, rows // 16)
+        def _(i):
+            r = pl.multiple_of(i * 16, 16)
+            full[z, pl.ds(pl.multiple_of(r + 8, 8), 16), LANES : LANES + cols] = dens[
+                z, pl.ds(r, 16), :
+            ].astype(jnp.float32)
 
     pl.semaphore_wait(
         barrier, bricks - 1 + jnp.where(has_low, 1, 0) + jnp.where(has_high, 1, 0)
@@ -126,18 +150,6 @@
     @pl.when(has_high)
     def _():
         halo_copy(1).start()
-
-    @pl.loop(0, stored)
-    def _(z):
-        full[z, 8 : 8 + rows, 0:LANES] = jnp.zeros((rows, LANES), jnp.float32)
-        full[z, 8 : 8 + rows, LANES + cols :] = jnp.zeros((rows, LANES), jnp.float32)
-
-        @pl.loop(0, rows // 16)
-        def _(i):
-            r = pl.multiple_of(i * 16, 16)
-            full[z, pl.ds(pl.multiple_of(r + 8, 8), 16), LANES : LANES + cols] = dens[
-                z, pl.ds(r, 16), :
-            ].astype(jnp.float32)
 
     def pixel_tile(r, c):
         def tile(z, dr, dc):
@@ -321,13 +333,12 @@
         strip = rows // bricks
         part = math.gcd(8, strip)
         blocks = strip // part
-        smem = pl.BlockSpec(memory_space=pltpu.SMEM)
         hbm = pl.BlockSpec(memory_space=pl.ANY)
         voxels = slices * rows * cols
         return pl.pallas_call(
             functools.partial(kernel, bricks, screens, strip),
             out_shape=jax.ShapeDtypeStruct((4, strip, cols), jnp.float32),
-            in_specs=[hbm, hbm, smem, smem, smem],
+            in_specs=[hbm] * 5,
             out_specs=pl.BlockSpec(memory_space=pltpu.VMEM),
             scratch_shapes=[
                 pltpu.VMEM((stored, rows, cols), jnp.bfloat16),
@@ -344,9 +355,13 @@
                 pltpu.SemaphoreType.DMA((bricks,)),
                 pltpu.SemaphoreType.DMA((bricks,)),
                 pltpu.SemaphoreType.DMA,
+                pltpu.SMEM((bricks,), jnp.int32),
+                pltpu.SMEM(color_table.shape[::-1], jnp.float32),
+                pltpu.SMEM(extinction.shape, jnp.float32),
+                pltpu.SemaphoreType.DMA((3,)),
             ],
             compiler_params=pltpu.CompilerParams(
-                collective_id=0, has_side_effects=True, vmem_limit_bytes=48 * 1024 * 1024
+                collective_id=0, has_side_effects=True, vmem_limit_bytes=64 * 1024 * 1024
             ),
             cost_estimate=pl.CostEstimate(
                 flops=60 * voxels, bytes_accessed=7 * voxels, transcendentals=3 * voxels

time: 39.5 us -> 34.2 us (0.87)
  local copies, waits for them, and re-layouts: 5.1 us -> 2.04 us
  Pallas kernels: 34.2 us -> 32 us
    unnamed x8 -> x0, local copies, waits for them, and re-layouts: 4.1 us -> none
    pallas_call x1, Pallas kernels: 34.2 us -> 32 us  [body(): pl.pallas_call(functools.partial(kernel, bricks, screens, strip), out_sha...]
    pallas_call x1, local copies, waits for them, and re-layouts: 1 us -> 2.04 us  [body(): pl.pallas_call(functools.partial(kernel, bricks, screens, strip), out_sha...]
where the time goes in v2:
time: 34.2 us; the launch traced here: 34 us
  Pallas kernels  32 us (94%)
  local copies, waits for them, and re-layouts  2.04 us (6%)
    pallas_call x1, Pallas kernels, body(): pl.pallas_call(functools.partial(kernel, bricks, screens, strip), out_sha...  32 us
    pallas_call x1, local copies, waits for them, and re-layouts, body(): pl.pallas_call(functools.partial(kernel, bricks, screens, strip), out_sha...  2.04 us

profile of v2, /device:TPU:1, one launch (start us, length us, event | category | flops | bytes accessed | tf_op | source)
XLA Modules:
  0.0 34.0 jit_solution(7935223429744904377)
XLA Ops:
  0.0 32.0 %shard_map.55 = f32[4,12,2048]{2,1,0:T(8,128)} custom-call(bf16[10,96,2048]{2,1,0:T(8,128)(2,1)} %dens_hbm.1, s32[8,96,2048]{2,1,0:T(8,128)} %mat_hbm.1, s32[8]{0:T(128)} %order_hbm.1, f32[3,16]{1,0:T(4,128)} %bitcast.1, f32[16]{0:T(128)} %ext_hbm.1), custom_call_target="tpu_custom_call" | custom-call | flops 94371840 | bytes 11010048 | tf_op jit(solution)/shard_map/pallas_call | solution.py:338
  32.0 2.0 %copy.6 = f32[4,12,2048]{2,0,1:T(4,128)} copy(f32[4,12,2048]{2,1,0:T(8,128)} %shard_map.55) | data formatting | bytes 786432 | tf_op jit(solution)/shard_map/pallas_call | solution.py:338

commit v3 on v2

--- a/solution.py
+++ b/solution.py
@@ -178,7 +178,9 @@
             def pick(values):
                 return jnp.take_along_axis(values, kinds, axis=1, mode="promise_in_bounds")
 
-            sigma = pick(ext2) * (here / (1.0 + here))
+            whole = 1.0 + here
+            guess = pl.reciprocal(whole, approx=True)
+            sigma = pick(ext2) * (here * (guess * (2.0 - whole * guess)))
             later = through * jnp.exp2(-sigma)
             weight = (through - later) * shade
             for k in range(3):
@@ -207,20 +209,41 @@
                             unit_at * (unit // part) + g * (8 // part) + h, p, :, pl.ds(c, LANES)
                         ] = words[p][h * part : (h + 1) * part]
 
-    def strip_copy(s):
+    def strip_copy(s, first=None, count=blocks):
+        first = s * blocks if first is None else first
         return pltpu.make_async_remote_copy(
-            src_ref=sendbuf.at[pl.ds(s * blocks, blocks)],
-            dst_ref=recv.at[me],
+            src_ref=sendbuf.at[pl.ds(first, count)],
+            dst_ref=recv.at[me, pl.ds(first - s * blocks, count)],
             send_sem=send_sem.at[s],
             recv_sem=recv_sem.at[me],
             device_id=(s, scr),
             device_id_type=MESH,
         )
 
-    def own_copy():
+    def own_copy(first, count):
         return pltpu.make_async_copy(
-            sendbuf.at[pl.ds(me * blocks, blocks)], recv.at[me], own_sem
-        )
+            sendbuf.at[pl.ds(first, count)],
+            recv.at[me, pl.ds(first - me * blocks, count)],
+            own_sem,
+        )
+
+    def pieces(group):
+        runs = {}
+        for b in range(group * (8 // part), (group + 1) * (8 // part)):
+            runs.setdefault(b // blocks, []).append(b)
+        return [(k, held[0], len(held)) for k, held in runs.items()]
+
+    def send(s, first, count, j):
+        if j < units - 1:
+            strip_copy(s, first, count).start()
+        else:
+            @pl.when(s != me)
+            def _():
+                strip_copy(s, first, count).start()
+
+            @pl.when(s == me)
+            def _():
+                own_copy(first, count).start()
 
     def set_halo(side, there):
         row = 7 if side == 0 else 8 + rows
@@ -252,20 +275,13 @@
             def _():
                 set_halo(1, has_high)
 
-            row_group(at, jnp.where(at == 0, groups - 1 - i, i))
-
-        for k in range(per_unit):
-            s = at * per_unit + k
-            if j < units - 1:
-                strip_copy(s).start()
-            else:
-                @pl.when(s != me)
+            g = jnp.where(at == 0, groups - 1 - i, i)
+            row_group(at, g)
+            for group in range(groups):
+                @pl.when(g == group)
                 def _():
-                    strip_copy(s).start()
-
-                @pl.when(s == me)
-                def _():
-                    own_copy().start()
+                    for k, first, count in pieces(group):
+                        send(at * per_unit + k, at * (unit // part) + first, count, j)
 
     def brick_at(rank):
         def step(j, found):
@@ -275,7 +291,7 @@
 
     at_rank = [brick_at(i) for i in range(bricks)]
 
-    own_copy().wait()
+    own_copy(me * blocks, blocks).wait()
     for peer in range(bricks):
         @pl.when(me != peer)
         def _():
@@ -308,7 +324,8 @@
                 sums = [a + weight * v for a, v in zip(sums, values[:3])]
                 through = later
             for k, value in enumerate(sums + [1.0 - through]):
-                out_ref[k, b * part : (b + 1) * part, where] = value
+                for row in range(part):
+                    out_ref[b * part + row, k : k + 1, where] = value[row : row + 1]
 
     for peer in range(bricks):
         @pl.when(me != peer)
@@ -335,9 +352,9 @@
         blocks = strip // part
         hbm = pl.BlockSpec(memory_space=pl.ANY)
         voxels = slices * rows * cols
-        return pl.pallas_call(
+        image = pl.pallas_call(
             functools.partial(kernel, bricks, screens, strip),
-            out_shape=jax.ShapeDtypeStruct((4, strip, cols), jnp.float32),
+            out_shape=jax.ShapeDtypeStruct((strip, 4, cols), jnp.float32),
             in_specs=[hbm] * 5,
             out_specs=pl.BlockSpec(memory_space=pltpu.VMEM),
             scratch_shapes=[
@@ -367,6 +384,7 @@
                 flops=60 * voxels, bytes_accessed=7 * voxels, transcendentals=3 * voxels
             ),
         )(density, material, order, color_table.T, extinction)
+        return image.transpose(1, 0, 2)
 
     placed = (P("depth", "screen", None), P("depth", "screen", None), P(), P(), P())
     return jax.shard_map(

time: 34.2 us -> 31.3 us (0.915)
  the two profiles are of different devices: /device:TPU:1 before, /device:TPU:0 now
where the time goes in v3:
time: 31.3 us; the launch traced here: 31.1 us
  Pallas kernels  29.3 us (94%)
  local copies, waits for them, and re-layouts  1.77 us (6%)
    pallas_call x1, Pallas kernels, body(): pl.pallas_call(functools.partial(kernel, bricks, screens, strip), out_sha...  29.3 us
    unnamed x1, local copies, waits for them, and re-layouts  1.77 us

profile of v3, /device:TPU:0, one launch (start us, length us, event | category | flops | bytes accessed | tf_op | source)
XLA Modules:
  0.0 31.1 jit_solution(9661687152746597226)
XLA Ops:
  0.0 29.3 %shard_map.55 = f32[12,4,2048]{2,1,0:T(4,128)} custom-call(bf16[10,96,2048]{2,1,0:T(8,128)(2,1)} %dens_hbm.1, s32[8,96,2048]{2,1,0:T(8,128)} %mat_hbm.1, s32[8]{0:T(128)} %order_hbm.1, f32[3,16]{1,0:T(4,128)} %bitcast.3, f32[16]{0:T(128)} %ext_hbm.1), custom_call_target="tpu_custom_call" | custom-call | flops 94371840 | bytes 11010048 | tf_op jit(solution)/shard_map/pallas_call | solution.py:355
  29.4 1.8 %copy.7 = f32[4,12,2048]{2,0,1:T(4,128)} copy(f32[4,12,2048]{2,0,1:T(4,128)} %bitcast.2) | data formatting | bytes 786432

commit v4 on v3

--- a/solution.py
+++ b/solution.py
@@ -27,7 +27,10 @@
     units = rows // unit
     groups = unit // 8
     per_unit = unit // strip
-    part = sendbuf.shape[2]
+    wide = sendbuf.shape[3]
+    fold = cols // wide
+    part = 8 // fold
+    runs = max(1, CHUNKS // fold)
     blocks = strip // part
     entries = ext_ref.shape[0]
 
@@ -42,13 +45,8 @@
     else:
         visits = [(own + 1 + j) % units for j in range(units)]
 
-    def dens_copy(h):
-        half = rows // 2
-        return pltpu.make_async_copy(
-            dens_hbm.at[:, pl.ds(h * half, half)],
-            dens.at[:, pl.ds(h * half, half)],
-            dens_sem.at[h],
-        )
+    def dens_copy(z):
+        return pltpu.make_async_copy(dens_hbm.at[z], dens.at[z], dens_sem.at[z])
 
     def mat_copy(j):
         where = pl.ds(pl.multiple_of(visits[j] * unit, 8), unit)
@@ -62,10 +60,9 @@
     ]
     for copy in small:
         copy.start()
-    for h in range(2):
-        dens_copy(h).start()
-    for j in range(units):
-        mat_copy(j).start()
+    for z in range(stored):
+        dens_copy(z).start()
+    mat_copy(0).start()
 
     barrier = pltpu.get_barrier_semaphore()
     for peer in range(bricks):
@@ -100,24 +97,24 @@
     steps = [jnp.broadcast_to(t * (1.0 / CODE_TOP), (8, LANES)) for t in tops + [top_tau]]
     scales = [1.0 / s for s in steps]
 
-    for h in range(2):
-        dens_copy(h).wait()
-
-    for z in range(slices):
-        halo_out[0, z : z + 1, :] = dens[z + 1, 0:16, :].astype(jnp.float32)[0:1]
-        halo_out[1, z : z + 1, :] = dens[z + 1, rows - 16 : rows, :].astype(jnp.float32)[15:16]
-
-    @pl.loop(0, stored)
-    def _(z):
+    for z in range(stored):
+        dens_copy(z).wait()
+        if z == stored - 1:
+            for j in range(1, units):
+                mat_copy(j).start()
         full[z, 8 : 8 + rows, 0:LANES] = jnp.zeros((rows, LANES), jnp.float32)
         full[z, 8 : 8 + rows, LANES + cols :] = jnp.zeros((rows, LANES), jnp.float32)
 
-        @pl.loop(0, rows // 16)
+        @pl.loop(0, rows // 32)
         def _(i):
-            r = pl.multiple_of(i * 16, 16)
-            full[z, pl.ds(pl.multiple_of(r + 8, 8), 16), LANES : LANES + cols] = dens[
-                z, pl.ds(r, 16), :
+            r = pl.multiple_of(i * 32, 32)
+            full[z, pl.ds(pl.multiple_of(r + 8, 8), 32), LANES : LANES + cols] = dens[
+                z, pl.ds(r, 32), :
             ].astype(jnp.float32)
+
+        if 0 < z <= slices:
+            halo_out[0, z - 1 : z, :] = full[z, 8:9, LANES : LANES + cols]
+            halo_out[1, z - 1 : z, :] = full[z, 7 + rows : 8 + rows, LANES : LANES + cols]
 
     pl.semaphore_wait(
         barrier, bricks - 1 + jnp.where(has_low, 1, 0) + jnp.where(has_high, 1, 0)
@@ -198,16 +195,17 @@
     def row_group(unit_at, g):
         r = pl.multiple_of(unit_at * unit + g * 8, 8)
 
-        @pl.loop(0, cols // (LANES * CHUNKS))
+        @pl.loop(0, wide // (LANES * runs))
         def _(i):
-            for k in range(CHUNKS):
-                c = pl.multiple_of(i * (LANES * CHUNKS) + k * LANES, LANES)
-                words = pixel_tile(r, c)
-                for p in range(2):
-                    for h in range(8 // part):
-                        sendbuf[
-                            unit_at * (unit // part) + g * (8 // part) + h, p, :, pl.ds(c, LANES)
-                        ] = words[p][h * part : (h + 1) * part]
+            for k in range(runs):
+                c = pl.multiple_of(i * (LANES * runs) + k * LANES, LANES)
+                tiles = [pixel_tile(r, pl.multiple_of(f * wide + c, LANES)) for f in range(fold)]
+                for h in range(fold):
+                    at = unit_at * (unit // part) + g * fold + h
+                    for p in range(2):
+                        sendbuf[at, p, :, pl.ds(c, LANES)] = jnp.concatenate(
+                            [words[p][h * part : (h + 1) * part] for words in tiles], axis=0
+                        )
 
     def strip_copy(s, first=None, count=blocks):
         first = s * blocks if first is None else first
@@ -304,14 +302,14 @@
                 device_id_type=MESH,
             ).wait_recv()
 
-    width = 4 * LANES
-    unscale = [jnp.concatenate([s[:part]] * (width // LANES), axis=1) for s in steps]
+    width = 2 * LANES
+    unscale = [jnp.concatenate([s] * (width // LANES), axis=1) for s in steps]
     for b in range(blocks):
-        @pl.loop(0, cols // width)
+        @pl.loop(0, wide // width)
         def _(i):
             where = pl.ds(pl.multiple_of(i * width, width), width)
-            through = jnp.ones((part, width), jnp.float32)
-            sums = [jnp.zeros((part, width), jnp.float32) for _ in range(3)]
+            through = jnp.ones((8, width), jnp.float32)
+            sums = [jnp.zeros((8, width), jnp.float32) for _ in range(3)]
             for rank in range(bricks):
                 first = recv[at_rank[rank], b, 0, :, where]
                 second = recv[at_rank[rank], b, 1, :, where]
@@ -324,8 +322,11 @@
                 sums = [a + weight * v for a, v in zip(sums, values[:3])]
                 through = later
             for k, value in enumerate(sums + [1.0 - through]):
-                for row in range(part):
-                    out_ref[b * part + row, k : k + 1, where] = value[row : row + 1]
+                for f in range(fold):
+                    to = pl.ds(pl.multiple_of(f * wide + i * width, width), width)
+                    for row in range(part):
+                        spot = f * part + row
+                        out_ref[b * part + row, k : k + 1, to] = value[spot : spot + 1]
 
     for peer in range(bricks):
         @pl.when(me != peer)
@@ -361,11 +362,11 @@
                 pltpu.VMEM((stored, rows, cols), jnp.bfloat16),
                 pltpu.VMEM((stored, rows + 16, cols + 2 * LANES), jnp.float32),
                 pltpu.VMEM((slices, rows, cols), jnp.int32),
-                pltpu.VMEM((rows // part, 2, part, cols), jnp.int32),
-                pltpu.VMEM((bricks, blocks, 2, part, cols), jnp.int32),
+                pltpu.VMEM((rows // part, 2, 8, cols * part // 8), jnp.int32),
+                pltpu.VMEM((bricks, blocks, 2, 8, cols * part // 8), jnp.int32),
                 pltpu.VMEM((2, slices, cols), jnp.float32),
                 pltpu.VMEM((2, slices, cols), jnp.float32),
-                pltpu.SemaphoreType.DMA((2,)),
+                pltpu.SemaphoreType.DMA((stored,)),
                 pltpu.SemaphoreType.DMA((rows // math.lcm(8, strip),)),
                 pltpu.SemaphoreType.DMA((2,)),
                 pltpu.SemaphoreType.DMA((2,)),

time: 31.3 us -> 31 us (level)
  no operation moved by 1% of the time
where the time goes in v4:
time: 31 us; the launch traced here: 30.8 us
  Pallas kernels  29 us (94%)
  local copies, waits for them, and re-layouts  1.77 us (6%)
    pallas_call x1, Pallas kernels, body(): pl.pallas_call(functools.partial(kernel, bricks, screens, strip), out_sha...  29 us
    unnamed x1, local copies, waits for them, and re-layouts  1.77 us

profile of v4, /device:TPU:0, one launch (start us, length us, event | category | flops | bytes accessed | tf_op | source)
XLA Modules:
  0.0 30.8 jit_solution(2525910745672167453)
XLA Ops:
  0.0 29.0 %shard_map.55 = f32[12,4,2048]{2,1,0:T(4,128)} custom-call(bf16[10,96,2048]{2,1,0:T(8,128)(2,1)} %dens_hbm.1, s32[8,96,2048]{2,1,0:T(8,128)} %mat_hbm.1, s32[8]{0:T(128)} %order_hbm.1, f32[3,16]{1,0:T(4,128)} %bitcast.3, f32[16]{0:T(128)} %ext_hbm.1), custom_call_target="tpu_custom_call" | custom-call | flops 94371840 | bytes 11010048 | tf_op jit(solution)/shard_map/pallas_call | solution.py:356
  29.0 1.8 %copy.7 = f32[4,12,2048]{2,0,1:T(4,128)} copy(f32[4,12,2048]{2,0,1:T(4,128)} %bitcast.2) | data formatting | bytes 786432

commit v5 on v4

--- a/solution.py
+++ b/solution.py
@@ -82,7 +82,6 @@
         copy.wait()
 
     lane = lax.broadcasted_iota(jnp.int32, (8, LANES), 1)
-    sub = lax.broadcasted_iota(jnp.int32, (8, LANES), 0)
 
     def table(read):
         out = jnp.zeros((8, LANES), jnp.float32)
@@ -102,19 +101,20 @@
         if z == stored - 1:
             for j in range(1, units):
                 mat_copy(j).start()
-        full[z, 8 : 8 + rows, 0:LANES] = jnp.zeros((rows, LANES), jnp.float32)
-        full[z, 8 : 8 + rows, LANES + cols :] = jnp.zeros((rows, LANES), jnp.float32)
+        for edge in (0, cols // LANES + 1):
+            full[z, edge, 8 : 8 + rows, :] = jnp.zeros((rows, LANES), jnp.float32)
 
         @pl.loop(0, rows // 32)
         def _(i):
             r = pl.multiple_of(i * 32, 32)
-            full[z, pl.ds(pl.multiple_of(r + 8, 8), 32), LANES : LANES + cols] = dens[
-                z, pl.ds(r, 32), :
-            ].astype(jnp.float32)
+            for k in range(cols // LANES):
+                full[z, 1 + k, pl.ds(pl.multiple_of(r + 8, 8), 32), :] = dens[
+                    z, pl.ds(r, 32), k * LANES : (k + 1) * LANES
+                ].astype(jnp.float32)
 
         if 0 < z <= slices:
-            halo_out[0, z - 1 : z, :] = full[z, 8:9, LANES : LANES + cols]
-            halo_out[1, z - 1 : z, :] = full[z, 7 + rows : 8 + rows, LANES : LANES + cols]
+            halo_out[0, z - 1 : z, :] = dens[z, 0:16, :].astype(jnp.float32)[0:1]
+            halo_out[1, z - 1 : z, :] = dens[z, rows - 16 : rows, :].astype(jnp.float32)[15:16]
 
     pl.semaphore_wait(
         barrier, bricks - 1 + jnp.where(has_low, 1, 0) + jnp.where(has_high, 1, 0)
@@ -148,12 +148,13 @@
     def _():
         halo_copy(1).start()
 
-    def pixel_tile(r, c):
+    def pixel_tile(r, chunk):
+        c = pl.multiple_of(chunk * LANES, LANES)
+
         def tile(z, dr, dc):
+            first = r + 8 + dr
             return full[
-                z,
-                pl.ds(pl.multiple_of(r + 8 + dr * 8, 8), 8),
-                pl.ds(pl.multiple_of(c + (1 + dc) * LANES, LANES), LANES),
+                z, chunk + 1 + dc, pl.ds(first if dr else pl.multiple_of(first, 8), 8), :
             ]
 
         through = jnp.ones((8, LANES), jnp.float32)
@@ -164,8 +165,8 @@
             after = tile(z + 2, 0, 0)
             left = pltpu.roll(jnp.where(lane == LANES - 1, tile(z + 1, 0, -1), here), 1, 1)
             right = pltpu.roll(jnp.where(lane == 0, tile(z + 1, 0, 1), here), LANES - 1, 1)
-            up = pltpu.roll(jnp.where(sub == 7, tile(z + 1, -1, 0), here), 1, 0)
-            down = pltpu.roll(jnp.where(sub == 0, tile(z + 1, 1, 0), here), 7, 0)
+            up = tile(z + 1, -1, 0)
+            down = tile(z + 1, 1, 0)
             dx, dy, dz = right - left, down - up, after - before
             square = (dx * dx + dy * dy) + (dz * dz + 4.0)
             lit = (0.45 * LIGHT[0]) * dx + (0.45 * LIGHT[1]) * dy + (0.45 * LIGHT[2]) * dz
@@ -199,7 +200,7 @@
         def _(i):
             for k in range(runs):
                 c = pl.multiple_of(i * (LANES * runs) + k * LANES, LANES)
-                tiles = [pixel_tile(r, pl.multiple_of(f * wide + c, LANES)) for f in range(fold)]
+                tiles = [pixel_tile(r, f * (wide // LANES) + i * runs + k) for f in range(fold)]
                 for h in range(fold):
                     at = unit_at * (unit // part) + g * fold + h
                     for p in range(2):
@@ -207,41 +208,32 @@
                             [words[p][h * part : (h + 1) * part] for words in tiles], axis=0
                         )
 
-    def strip_copy(s, first=None, count=blocks):
-        first = s * blocks if first is None else first
+    def block_copy(s, b):
         return pltpu.make_async_remote_copy(
-            src_ref=sendbuf.at[pl.ds(first, count)],
-            dst_ref=recv.at[me, pl.ds(first - s * blocks, count)],
-            send_sem=send_sem.at[s],
-            recv_sem=recv_sem.at[me],
+            src_ref=sendbuf.at[s * blocks + b],
+            dst_ref=recv[b].at[me],
+            send_sem=send_sem.at[s, b],
+            recv_sem=recv_sem.at[me, b],
             device_id=(s, scr),
             device_id_type=MESH,
         )
 
-    def own_copy(first, count):
+    def own_copy(b):
         return pltpu.make_async_copy(
-            sendbuf.at[pl.ds(first, count)],
-            recv.at[me, pl.ds(first - me * blocks, count)],
-            own_sem,
+            sendbuf.at[me * blocks + b], recv[b].at[me], own_sem.at[b]
         )
 
-    def pieces(group):
-        runs = {}
-        for b in range(group * (8 // part), (group + 1) * (8 // part)):
-            runs.setdefault(b // blocks, []).append(b)
-        return [(k, held[0], len(held)) for k, held in runs.items()]
-
-    def send(s, first, count, j):
+    def send(s, b, j):
         if j < units - 1:
-            strip_copy(s, first, count).start()
+            block_copy(s, b).start()
         else:
             @pl.when(s != me)
             def _():
-                strip_copy(s, first, count).start()
+                block_copy(s, b).start()
 
             @pl.when(s == me)
             def _():
-                own_copy(first, count).start()
+                own_copy(b).start()
 
     def set_halo(side, there):
         row = 7 if side == 0 else 8 + rows
@@ -250,14 +242,16 @@
         def _():
             halo_wait(side)
             for z in range(slices):
-                full[z + 1, row : row + 1, LANES : LANES + cols] = halo_in[side, z : z + 1, :]
+                for k in range(cols // LANES):
+                    full[z + 1, 1 + k, row : row + 1, :] = halo_in[
+                        side, z : z + 1, k * LANES : (k + 1) * LANES
+                    ]
 
         @pl.when(jnp.logical_not(there))
         def _():
             for z in range(slices):
-                full[z + 1, row : row + 1, LANES : LANES + cols] = jnp.zeros(
-                    (1, cols), jnp.float32
-                )
+                for k in range(cols // LANES):
+                    full[z + 1, 1 + k, row : row + 1, :] = jnp.zeros((1, LANES), jnp.float32)
 
     for j in range(units):
         at = visits[j]
@@ -278,8 +272,8 @@
             for group in range(groups):
                 @pl.when(g == group)
                 def _():
-                    for k, first, count in pieces(group):
-                        send(at * per_unit + k, at * (unit // part) + first, count, j)
+                    for b in range(group * fold, (group + 1) * fold):
+                        send(at * per_unit + b // blocks, b % blocks, j)
 
     def brick_at(rank):
         def step(j, found):
@@ -289,30 +283,30 @@
 
     at_rank = [brick_at(i) for i in range(bricks)]
 
-    own_copy(me * blocks, blocks).wait()
-    for peer in range(bricks):
-        @pl.when(me != peer)
-        def _():
-            pltpu.make_async_remote_copy(
-                src_ref=sendbuf.at[pl.ds(peer * blocks, blocks)],
-                dst_ref=recv.at[peer],
-                send_sem=send_sem.at[peer],
-                recv_sem=recv_sem.at[peer],
-                device_id=(peer, scr),
-                device_id_type=MESH,
-            ).wait_recv()
-
     width = 2 * LANES
     unscale = [jnp.concatenate([s] * (width // LANES), axis=1) for s in steps]
     for b in range(blocks):
+        own_copy(b).wait()
+        for peer in range(bricks):
+            @pl.when(me != peer)
+            def _():
+                pltpu.make_async_remote_copy(
+                    src_ref=sendbuf.at[peer * blocks + b],
+                    dst_ref=recv[b].at[peer],
+                    send_sem=send_sem.at[peer, b],
+                    recv_sem=recv_sem.at[peer, b],
+                    device_id=(peer, scr),
+                    device_id_type=MESH,
+                ).wait_recv()
+
         @pl.loop(0, wide // width)
         def _(i):
             where = pl.ds(pl.multiple_of(i * width, width), width)
             through = jnp.ones((8, width), jnp.float32)
             sums = [jnp.zeros((8, width), jnp.float32) for _ in range(3)]
             for rank in range(bricks):
-                first = recv[at_rank[rank], b, 0, :, where]
-                second = recv[at_rank[rank], b, 1, :, where]
+                first = recv[b][at_rank[rank], 0, :, where]
+                second = recv[b][at_rank[rank], 1, :, where]
                 codes = []
                 for word in (first, second):
                     codes += [lax.shift_right_logical(word, 16), word & 0xFFFF]
@@ -331,7 +325,8 @@
     for peer in range(bricks):
         @pl.when(me != peer)
         def _():
-            strip_copy(peer).wait_send()
+            for b in range(blocks):
+                block_copy(peer, b).wait_send()
 
     @pl.when(has_low)
     def _():
@@ -360,19 +355,19 @@
             out_specs=pl.BlockSpec(memory_space=pltpu.VMEM),
             scratch_shapes=[
                 pltpu.VMEM((stored, rows, cols), jnp.bfloat16),
-                pltpu.VMEM((stored, rows + 16, cols + 2 * LANES), jnp.float32),
+                pltpu.VMEM((stored, cols // LANES + 2, rows + 16, LANES), jnp.float32),
                 pltpu.VMEM((slices, rows, cols), jnp.int32),
                 pltpu.VMEM((rows // part, 2, 8, cols * part // 8), jnp.int32),
-                pltpu.VMEM((bricks, blocks, 2, 8, cols * part // 8), jnp.int32),
+                [pltpu.VMEM((bricks, 2, 8, cols * part // 8), jnp.int32)] * blocks,
                 pltpu.VMEM((2, slices, cols), jnp.float32),
                 pltpu.VMEM((2, slices, cols), jnp.float32),
                 pltpu.SemaphoreType.DMA((stored,)),
                 pltpu.SemaphoreType.DMA((rows // math.lcm(8, strip),)),
                 pltpu.SemaphoreType.DMA((2,)),
                 pltpu.SemaphoreType.DMA((2,)),
-                pltpu.SemaphoreType.DMA((bricks,)),
-                pltpu.SemaphoreType.DMA((bricks,)),
-                pltpu.SemaphoreType.DMA,
+                pltpu.SemaphoreType.DMA((bricks, blocks)),
+                pltpu.SemaphoreType.DMA((bricks, blocks)),
+                pltpu.SemaphoreType.DMA((blocks,)),
                 pltpu.SMEM((bricks,), jnp.int32),
                 pltpu.SMEM(color_table.shape[::-1], jnp.float32),
                 pltpu.SMEM(extinction.shape, jnp.float32),

time: 31 us -> 31.1 us (level)
  no operation moved by 1% of the time
where the time goes in v5:
time: 31.1 us; the launch traced here: 31 us
  Pallas kernels  29.2 us (94%)
  local copies, waits for them, and re-layouts  1.77 us (6%)
    pallas_call x1, Pallas kernels, body(): pl.pallas_call(functools.partial(kernel, bricks, screens, strip), out_sha...  29.2 us
    unnamed x1, local copies, waits for them, and re-layouts  1.77 us

profile of v5, /device:TPU:0, one launch (start us, length us, event | category | flops | bytes accessed | tf_op | source)
XLA Modules:
  0.0 31.0 jit_solution(8761847447088351067)
XLA Ops:
  0.0 29.2 %shard_map.55 = f32[12,4,2048]{2,1,0:T(4,128)} custom-call(bf16[10,96,2048]{2,1,0:T(8,128)(2,1)} %dens_hbm.1, s32[8,96,2048]{2,1,0:T(8,128)} %mat_hbm.1, s32[8]{0:T(128)} %order_hbm.1, f32[3,16]{1,0:T(4,128)} %bitcast.3, f32[16]{0:T(128)} %ext_hbm.1), custom_call_target="tpu_custom_call" | custom-call | flops 94371840 | bytes 11010048 | tf_op jit(solution)/shard_map/pallas_call | solution.py:351
  29.2 1.8 %copy.7 = f32[4,12,2048]{2,0,1:T(4,128)} copy(f32[4,12,2048]{2,0,1:T(4,128)} %bitcast.2) | data formatting | bytes 786432

commit v6 on v4

--- a/solution.py
+++ b/solution.py
@@ -41,7 +41,9 @@
 
     own = (me * strip) // unit
     if units == 4:
-        visits = [3 - own, own + 1 - 2 * (own % 2), (own + 2) % 4, own]
+        across, along = own + 1 - 2 * (own % 2), (own + 2) % 4
+        even = me % 2 == 0
+        visits = [3 - own, jnp.where(even, across, along), jnp.where(even, along, across), own]
     else:
         visits = [(own + 1 + j) % units for j in range(units)]
 
@@ -97,6 +99,23 @@
     steps = [jnp.broadcast_to(t * (1.0 / CODE_TOP), (8, LANES)) for t in tops + [top_tau]]
     scales = [1.0 / s for s in steps]
 
+    early = 1 if units == 4 and rows == 96 else 0
+    upper = visits[0] >= 2
+
+    def convert(z, skip, count):
+        @pl.loop(0, count)
+        def _(i):
+            if skip == 0 and early == 0:
+                r = i * 32
+            elif skip:
+                r = jnp.where(upper, 32, 0) + i * 32
+            else:
+                r = jnp.where(upper, 0, 64) + i * 32
+            r = pl.multiple_of(r, 32)
+            full[z, pl.ds(pl.multiple_of(r + 8, 8), 32), LANES : LANES + cols] = dens[
+                z, pl.ds(r, 32), :
+            ].astype(jnp.float32)
+
     for z in range(stored):
         dens_copy(z).wait()
         if z == stored - 1:
@@ -105,16 +124,10 @@
         full[z, 8 : 8 + rows, 0:LANES] = jnp.zeros((rows, LANES), jnp.float32)
         full[z, 8 : 8 + rows, LANES + cols :] = jnp.zeros((rows, LANES), jnp.float32)
 
-        @pl.loop(0, rows // 32)
-        def _(i):
-            r = pl.multiple_of(i * 32, 32)
-            full[z, pl.ds(pl.multiple_of(r + 8, 8), 32), LANES : LANES + cols] = dens[
-                z, pl.ds(r, 32), :
-            ].astype(jnp.float32)
-
+        convert(z, 64 * early, rows // 32 - early)
         if 0 < z <= slices:
-            halo_out[0, z - 1 : z, :] = full[z, 8:9, LANES : LANES + cols]
-            halo_out[1, z - 1 : z, :] = full[z, 7 + rows : 8 + rows, LANES : LANES + cols]
+            halo_out[0, z - 1 : z, :] = dens[z, 0:16, :].astype(jnp.float32)[0:1]
+            halo_out[1, z - 1 : z, :] = dens[z, rows - 16 : rows, :].astype(jnp.float32)[15:16]
 
     pl.semaphore_wait(
         barrier, bricks - 1 + jnp.where(has_low, 1, 0) + jnp.where(has_high, 1, 0)
@@ -262,6 +275,10 @@
     for j in range(units):
         at = visits[j]
         mat_copy(j).wait()
+        if j == 1 and early:
+            @pl.loop(0, stored)
+            def _(z):
+                convert(z, 0, 1)
 
         @pl.loop(0, groups)
         def _(i):
@@ -379,7 +396,7 @@
                 pltpu.SemaphoreType.DMA((3,)),
             ],
             compiler_params=pltpu.CompilerParams(
-                collective_id=0, has_side_effects=True, vmem_limit_bytes=64 * 1024 * 1024
+                collective_id=0, has_side_effects=True, vmem_limit_bytes=62 * 1024 * 1024
             ),
             cost_estimate=pl.CostEstimate(
                 flops=60 * voxels, bytes_accessed=7 * voxels, transcendentals=3 * voxels

time: 31 us -> 30.5 us (0.984)
  Pallas kernels: 29 us -> 28.6 us
    pallas_call x1, Pallas kernels: 29 us -> 28.6 us  [body(): pl.pallas_call(functools.partial(kernel, bricks, screens, strip), out_sha...]
where the time goes in v6:
time: 30.5 us; the launch traced here: 30.4 us
  Pallas kernels  28.6 us (94%)
  local copies, waits for them, and re-layouts  1.77 us (6%)
    pallas_call x1, Pallas kernels, body(): pl.pallas_call(functools.partial(kernel, bricks, screens, strip), out_sha...  28.6 us
    unnamed x1, local copies, waits for them, and re-layouts  1.77 us

profile of v6, /device:TPU:0, one launch (start us, length us, event | category | flops | bytes accessed | tf_op | source)
XLA Modules:
  0.0 30.4 jit_solution(16034360470116567658)
XLA Ops:
  0.0 28.6 %shard_map.55 = f32[12,4,2048]{2,1,0:T(4,128)} custom-call(bf16[10,96,2048]{2,1,0:T(8,128)(2,1)} %dens_hbm.1, s32[8,96,2048]{2,1,0:T(8,128)} %mat_hbm.1, s32[8]{0:T(128)} %order_hbm.1, f32[3,16]{1,0:T(4,128)} %bitcast.3, f32[16]{0:T(128)} %ext_hbm.1), custom_call_target="tpu_custom_call" | custom-call | flops 94371840 | bytes 11010048 | tf_op jit(solution)/shard_map/pallas_call | solution.py:373
  28.6 1.8 %copy.7 = f32[4,12,2048]{2,0,1:T(4,128)} copy(f32[4,12,2048]{2,0,1:T(4,128)} %bitcast.2) | data formatting | bytes 786432

commit v7 on v6

--- a/solution.py
+++ b/solution.py
@@ -11,7 +11,7 @@
 MESH = pl.DeviceIdType.MESH
 LANES = 128
 CODE_TOP = 65000.0
-CHUNKS = 4
+CHUNKS = 8
 
 
 def kernel(
@@ -93,11 +93,15 @@
         return out
 
     tabs = [table(lambda e, c=c: color_ref[c, e]) for c in range(3)]
+    slope = 0.45 * LIGHT[2]
     ext2 = table(lambda e: ext_ref[e]) * math.log2(math.e)
     tops = [jnp.max(t, axis=1, keepdims=True) for t in tabs]
     top_tau = slices * jnp.max(ext2, axis=1, keepdims=True)
     steps = [jnp.broadcast_to(t * (1.0 / CODE_TOP), (8, LANES)) for t in tops + [top_tau]]
     scales = [1.0 / s for s in steps]
+    scales[3] = -scales[3]
+    scaled = [t * slope for t in tabs]
+    minus_ext2 = -ext2
 
     early = 1 if units == 4 and rows == 96 else 0
     upper = visits[0] >= 2
@@ -181,8 +185,8 @@
             down = pltpu.roll(jnp.where(sub == 0, tile(z + 1, 1, 0), here), 7, 0)
             dx, dy, dz = right - left, down - up, after - before
             square = (dx * dx + dy * dy) + (dz * dz + 4.0)
-            lit = (0.45 * LIGHT[0]) * dx + (0.45 * LIGHT[1]) * dy + (0.45 * LIGHT[2]) * dz
-            shade = 0.55 + lit * lax.rsqrt(square)
+            lit = (LIGHT[0] / LIGHT[2]) * dx + (LIGHT[1] / LIGHT[2]) * dy + dz
+            shade = (0.55 / slope) + lit * lax.rsqrt(square)
             kinds = mat[z, pl.ds(r, 8), pl.ds(c, LANES)]
 
             def pick(values):
@@ -190,19 +194,19 @@
 
             whole = 1.0 + here
             guess = pl.reciprocal(whole, approx=True)
-            sigma = pick(ext2) * (here * (guess * (2.0 - whole * guess)))
-            later = through * jnp.exp2(-sigma)
+            sigma = pick(minus_ext2) * (here * (guess * (2.0 - whole * guess)))
+            later = through * jnp.exp2(sigma)
             weight = (through - later) * shade
             for k in range(3):
-                sums[k] = sums[k] + weight * pick(tabs[k])
+                sums[k] = sums[k] + weight * pick(scaled[k])
             tau = tau + sigma
             through = later
             before, here = here, after
-        gain = 1.0 / (1.0 - through)
+        dark = 1.0 - through
+        gain = pl.reciprocal(dark, approx=True)
+        gain = gain * (2.0 - dark * gain)
         values = [s * gain for s in sums] + [tau]
-        codes = [
-            jnp.minimum(v * s + 0.5, 65535.0).astype(jnp.int32) for v, s in zip(values, scales)
-        ]
+        codes = [(v * s + 0.5).astype(jnp.int32) for v, s in zip(values, scales)]
         return [(codes[0] << 16) | codes[1], (codes[2] << 16) | codes[3]]
 
     def row_group(unit_at, g):

time: 30.5 us -> 29.6 us (0.970)
  Pallas kernels: 28.6 us -> 27.6 us
    pallas_call x1, Pallas kernels: 28.6 us -> 27.6 us  [body(): pl.pallas_call(functools.partial(kernel, bricks, screens, strip), out_sha...]
where the time goes in v7:
time: 29.6 us; the launch traced here: 29.4 us
  Pallas kernels  27.6 us (93%)
  local copies, waits for them, and re-layouts  1.77 us (6%)
    pallas_call x1, Pallas kernels, body(): pl.pallas_call(functools.partial(kernel, bricks, screens, strip), out_sha...  27.6 us
    unnamed x1, local copies, waits for them, and re-layouts  1.77 us

profile of v7, /device:TPU:0, one launch (start us, length us, event | category | flops | bytes accessed | tf_op | source)
XLA Modules:
  0.0 29.4 jit_solution(2344064761494546581)
XLA Ops:
  0.0 27.6 %shard_map.55 = f32[12,4,2048]{2,1,0:T(4,128)} custom-call(bf16[10,96,2048]{2,1,0:T(8,128)(2,1)} %dens_hbm.1, s32[8,96,2048]{2,1,0:T(8,128)} %mat_hbm.1, s32[8]{0:T(128)} %order_hbm.1, f32[3,16]{1,0:T(4,128)} %bitcast.3, f32[16]{0:T(128)} %ext_hbm.1), custom_call_target="tpu_custom_call" | custom-call | flops 94371840 | bytes 11010048 | tf_op jit(solution)/shard_map/pallas_call | solution.py:377
  27.6 1.8 %copy.7 = f32[4,12,2048]{2,0,1:T(4,128)} copy(f32[4,12,2048]{2,0,1:T(4,128)} %bitcast.2) | data formatting | bytes 786432
